TPU v7x, 32 devices: a whole 2x2x4 slice. The times are simulated.
32 devices in a mesh: dp: 16 (over z, x, core), tensor: 2 (over y).
Axes of the slice: x: 2, y: 2, z: 4, core: 2. Of those that a mesh axis runs over, the one named last changes fastest.
Arguments:
- inputs: bfloat16 [40960, 1024], P(('dp', 'tensor')), may hold values from -6 to 6
- teacher: bfloat16 [40960, 1024], P(('dp', 'tensor')), may hold values from -6 to 6
- lengths: int32 [128], replicated, may hold values from 200 to 320, as said below
- first_gain: float32 [1024], replicated, may hold values from 0.5 to 1.5
- first_shift: float32 [1024], replicated, may hold values from -0.2 to 0.2
- query_key_value_weight: bfloat16 [3, 1024, 1024], P(None, 'dp', 'tensor'), may hold values from -0.1875 to 0.1875
- heads_bias: float32 [2, 1024], P(None, 'tensor'), may hold values from -0.2 to 0.2
- merge_weight: bfloat16 [1024, 1024], P('dp', 'tensor'), may hold values from -1.5 to 1.5
- merge_bias: float32 [1024], replicated, may hold values from -0.6 to 0.6
- second_gain: float32 [1024], replicated, may hold values from 0.5 to 1.5
- second_shift: float32 [1024], replicated, may hold values from -0.6 to 0.6
- expand_weight: bfloat16 [1024, 4096], P('dp', 'tensor'), may hold values from -0.1875 to 0.1875
- expand_bias: float32 [4096], P('tensor'), may hold values from -0.6 to 0.6
- reduce_weight: bfloat16 [1024, 4096], P('dp', 'tensor'), may hold values from -0.09375 to 0.09375
- reduce_bias: float32 [1024], replicated, may hold values from -0.6 to 0.6
Outputs:
- loss_value: float32 [], replicated
- outputs: bfloat16 [40960, 1024], P(('dp', 'tensor'))
- inputs_grad: float32 [40960, 1024], P(('dp', 'tensor'))
- first_gain_grad: float32 [1024], replicated
- first_shift_grad: float32 [1024], replicated
- heads_weight_grad: float32 [3, 1024, 1024], P(None, 'dp', 'tensor')
- heads_bias_grad: float32 [2, 1024], P(None, 'tensor')
- merge_weight_grad: float32 [1024, 1024], P('dp', 'tensor')
- merge_bias_grad: float32 [1024], replicated
- second_gain_grad: float32 [1024], replicated
- second_shift_grad: float32 [1024], replicated
- expand_weight_grad: float32 [1024, 4096], P('dp', 'tensor')
- expand_bias_grad: float32 [4096], P('tensor')
- reduce_weight_grad: float32 [1024, 4096], P('dp', 'tensor')
- reduce_bias_grad: float32 [1024], replicated
Inputs may be any that keep to these rules, and one draw needn't show every extreme that they name: `lengths`: in every draw some image has all 320 slots valid.
All inputs are finite; a program needn't handle non-finite values.
Results may differ from a plain program's by a relative error of at most 0.0095.
Values may be sent and summed in bfloat16 or wider, within the bound.
A program may use at most 320 MiB of HBM per device.

v0:
```python
from functools import partial
import math
import jax
import jax.numpy as jnp
from jax import lax
from jax.sharding import PartitionSpec as P

HD = 64
SLOTS = 320
EPSILON = 1e-05
MASKED_SCORE = -1e30


def layer_norm(rows, gain, shift):
    centre = jnp.mean(rows, axis=-1, keepdims=True)
    centred = rows - centre
    spread = jnp.mean(centred * centred, axis=-1, keepdims=True)
    return centred * lax.rsqrt(spread + EPSILON) * gain + shift


def gather_rows(values):
    return lax.all_gather(values, "tensor", axis=0, tiled=True)


def reduce_rows(values):
    return lax.psum_scatter(values, "tensor", scatter_dimension=0, tiled=True)


def fetch_mixing(query_key_value_weight, merge_weight):
    return (
        lax.all_gather(query_key_value_weight, "dp", axis=1, tiled=True),
        lax.all_gather(merge_weight, "dp", axis=0, tiled=True),
    )


def fetch_feed(expand_weight, reduce_weight):
    return (
        lax.all_gather(expand_weight, "dp", axis=0, tiled=True),
        lax.all_gather(reduce_weight, "dp", axis=0, tiled=True),
    )


def masked_scores(query_heads, key_heads, key_valid, scale):
    raw_scores = (
        jnp.einsum("bqhe,bkhe->bhqk", query_heads, key_heads, preferred_element_type=jnp.float32)
        * scale
    )
    return jnp.where(key_valid[:, None, None, :], raw_scores, MASKED_SCORE)


def body(
    inputs,
    teacher,
    lengths,
    first_gain,
    first_shift,
    query_key_value_weight,
    heads_bias,
    merge_weight,
    merge_bias,
    second_gain,
    second_shift,
    expand_weight,
    expand_bias,
    reduce_weight,
    reduce_bias,
):
    local_rows = inputs.shape[0]
    group_rows = local_rows * lax.axis_size("tensor")
    images = group_rows // SLOTS
    local_width = query_key_value_weight.shape[2]
    local_heads = local_width // HD
    scale = 1.0 / math.sqrt(HD)
    mine = lax.dynamic_slice_in_dim(lengths, lax.axis_index("dp") * images, images)
    key_valid = jnp.arange(SLOTS, dtype=jnp.int32)[None, :] < mine[:, None]
    row_valid = lax.dynamic_slice_in_dim(
        key_valid.reshape(group_rows), lax.axis_index("tensor") * local_rows, local_rows
    )
    row_valid = row_valid.astype(jnp.float32)[:, None]
    count = jnp.sum(lengths).astype(jnp.float32)
    inputs_f = inputs.astype(jnp.float32)
    normalized_rows, first_back = jax.vjp(layer_norm, inputs_f, first_gain, first_shift)
    normed_b = normalized_rows.astype(jnp.bfloat16)
    normalized_complete = gather_rows(normed_b)
    heads_complete_rows, merge_full = fetch_mixing(query_key_value_weight, merge_weight)
    projected_heads = jnp.einsum(
        "xz,ezi->exi", normalized_complete, heads_complete_rows, preferred_element_type=jnp.float32
    )
    queries = (projected_heads[0] + heads_bias[0]).astype(jnp.bfloat16)
    key_rows = projected_heads[1].astype(jnp.bfloat16)
    value_rows = (projected_heads[2] + heads_bias[1]).astype(jnp.bfloat16)
    query_heads = queries.reshape(images, SLOTS, local_heads, HD)
    key_heads = key_rows.reshape(images, SLOTS, local_heads, HD)
    value_heads = value_rows.reshape(images, SLOTS, local_heads, HD)
    scores = masked_scores(query_heads, key_heads, key_valid, scale)
    highest = jnp.max(scores, axis=-1, keepdims=True)
    expo = jnp.exp(scores - highest)
    totals = jnp.sum(expo, axis=-1, keepdims=True)
    attend = expo / totals
    log_total = highest + jnp.log(totals)
    mixed = jnp.einsum(
        "bhqk,bkhe->bqhe",
        attend.astype(jnp.bfloat16),
        value_heads,
        preferred_element_type=jnp.float32,
    )
    mixed_b = mixed.reshape(group_rows, local_width).astype(jnp.bfloat16)
    branch_part = jnp.einsum("rf,df->rd", mixed_b, merge_full, preferred_element_type=jnp.float32)
    hidden_state = inputs_f + reduce_rows(branch_part) + merge_bias
    second, second_back = jax.vjp(layer_norm, hidden_state, second_gain, second_shift)
    second_b = second.astype(jnp.bfloat16)
    second_full = gather_rows(second_b)
    expand_full, reduce_full = fetch_feed(expand_weight, reduce_weight)
    pre_act = jnp.dot(second_full, expand_full, preferred_element_type=jnp.float32) + expand_bias
    activ, gelu_back = jax.vjp(partial(jax.nn.gelu, approximate=True), pre_act)
    activ_b = activ.astype(jnp.bfloat16)
    feed_part = jnp.einsum("rf,df->rd", activ_b, reduce_full, preferred_element_type=jnp.float32)
    feed_sum = reduce_rows(feed_part)
    result = (hidden_state + feed_sum + reduce_bias) * row_valid
    error = (result - teacher.astype(jnp.float32)) * row_valid
    loss_part = jnp.sum(error * error)
    result_grad = 2.0 * error / count
    expand_back, reduce_back = fetch_feed(expand_weight, reduce_weight)
    second_src = gather_rows(second_b)
    result_full = gather_rows(result_grad.astype(jnp.bfloat16))
    activ_grad = jnp.dot(result_full, reduce_back, preferred_element_type=jnp.float32)
    reduce_grad = jnp.einsum("rd,rf->df", result_full, activ_b, preferred_element_type=jnp.float32)
    pre_grad = gelu_back(activ_grad)[0].astype(jnp.bfloat16)
    expand_bias_grad = jnp.sum(pre_grad, axis=0, dtype=jnp.float32)
    expand_grad = jnp.einsum("rd,rf->df", second_src, pre_grad, preferred_element_type=jnp.float32)
    second_grad = reduce_rows(
        jnp.einsum("rf,df->rd", pre_grad, expand_back, preferred_element_type=jnp.float32)
    )
    hidden_ln_grad, second_gain_grad, second_shift_grad = second_back(second_grad)
    hidden_grad = result_grad + hidden_ln_grad
    reduce_bias_grad = jnp.sum(result_grad, axis=0)
    merge_bias_grad = jnp.sum(hidden_grad, axis=0)
    heads_pullback_rows, merge_back = fetch_mixing(query_key_value_weight, merge_weight)
    normalized_input_rows = gather_rows(normed_b)
    hidden_full = gather_rows(hidden_grad.astype(jnp.bfloat16))
    mixed_grad = jnp.einsum(
        "rd,df->rf", hidden_full, merge_back, preferred_element_type=jnp.float32
    ).astype(jnp.bfloat16)
    merge_grad = jnp.einsum("rd,rf->df", hidden_full, mixed_b, preferred_element_type=jnp.float32)
    mixed_heads = mixed_grad.reshape(images, SLOTS, local_heads, HD)
    attend_again = jnp.exp(masked_scores(query_heads, key_heads, key_valid, scale) - log_total)
    value_grad = jnp.einsum(
        "bhqk,bqhe->bkhe",
        attend_again.astype(jnp.bfloat16),
        mixed_heads,
        preferred_element_type=jnp.float32,
    ).astype(jnp.bfloat16)
    attend_grad = jnp.einsum(
        "bqhe,bkhe->bhqk", mixed_heads, value_heads, preferred_element_type=jnp.float32
    )
    score_grad = attend_again * (
        attend_grad - jnp.sum(attend_again * attend_grad, axis=-1, keepdims=True)
    )
    score_grad = score_grad.astype(jnp.bfloat16)
    query_grad = (
        jnp.einsum("bhqk,bkhe->bqhe", score_grad, key_heads, preferred_element_type=jnp.float32)
        * scale
    ).astype(jnp.bfloat16)
    key_grad = (
        jnp.einsum("bhqk,bqhe->bkhe", score_grad, query_heads, preferred_element_type=jnp.float32)
        * scale
    ).astype(jnp.bfloat16)
    projected_heads_gradient = jnp.stack(
        [
            query_grad.reshape(group_rows, local_width),
            key_grad.reshape(group_rows, local_width),
            value_grad.reshape(group_rows, local_width),
        ]
    )
    heads_bias_grad = jnp.stack(
        [
            jnp.sum(projected_heads_gradient[0], axis=0, dtype=jnp.float32),
            jnp.sum(projected_heads_gradient[2], axis=0, dtype=jnp.float32),
        ]
    )
    heads_grad = jnp.einsum(
        "jb,mjx->mbx",
        normalized_input_rows,
        projected_heads_gradient,
        preferred_element_type=jnp.float32,
    )
    normed_grad = reduce_rows(
        jnp.einsum(
            "mex,mwx->ew",
            projected_heads_gradient,
            heads_pullback_rows,
            preferred_element_type=jnp.float32,
        )
    )
    inputs_ln_grad, first_gain_grad, first_shift_grad = first_back(normed_grad)
    inputs_grad = hidden_grad + inputs_ln_grad
    heads_grad, merge_grad = (
        lax.psum_scatter(
            heads_grad.astype(jnp.bfloat16), "dp", scatter_dimension=1, tiled=True
        ).astype(jnp.float32),
        lax.psum_scatter(
            merge_grad.astype(jnp.bfloat16), "dp", scatter_dimension=0, tiled=True
        ).astype(jnp.float32),
    )
    expand_grad, reduce_grad = (
        lax.psum_scatter(
            expand_grad.astype(jnp.bfloat16), "dp", scatter_dimension=0, tiled=True
        ).astype(jnp.float32),
        lax.psum_scatter(
            reduce_grad.astype(jnp.bfloat16), "dp", scatter_dimension=0, tiled=True
        ).astype(jnp.float32),
    )
    heads_bias_grad, expand_bias_grad = lax.psum((heads_bias_grad, expand_bias_grad), "dp")
    summed = lax.psum(
        (
            first_gain_grad,
            first_shift_grad,
            second_gain_grad,
            second_shift_grad,
            merge_bias_grad,
            reduce_bias_grad,
            loss_part,
        ),
        ("dp", "tensor"),
    )
    loss_value = summed[6] / count
    return (
        loss_value,
        result.astype(jnp.bfloat16),
        inputs_grad,
        summed[0],
        summed[1],
        heads_grad,
        heads_bias_grad,
        merge_grad,
        summed[4],
        summed[2],
        summed[3],
        expand_grad,
        expand_bias_grad,
        reduce_grad,
        summed[5],
    )


def solution(mesh):
    return jax.shard_map(
        body,
        mesh=mesh,
        in_specs=(
            P(("dp", "tensor"), None),
            P(("dp", "tensor"), None),
            P(),
            P(),
            P(),
            P(None, "dp", "tensor"),
            P(None, "tensor"),
            P("dp", "tensor"),
            P(),
            P(),
            P(),
            P("dp", "tensor"),
            P("tensor"),
            P("dp", "tensor"),
            P(),
        ),
        out_specs=(
            P(),
            P(("dp", "tensor"), None),
            P(("dp", "tensor"), None),
            P(),
            P(),
            P(None, "dp", "tensor"),
            P(None, "tensor"),
            P("dp", "tensor"),
            P(),
            P(),
            P(),
            P("dp", "tensor"),
            P("tensor"),
            P("dp", "tensor"),
            P(),
        ),
        check_vma=False,
    )
```

profile of v0, /device:TPU:0, one launch (start us, length us, event | category | flops | bytes accessed | tf_op | source)
XLA Modules:
  0.0 1575.8 jit_solution(5867062736825207133)
XLA Ops:
  17.6 69.5 %all-gather.9.cloned.1.call-done = bf16[2560,1024]{1,0:T(8,128)(2,1)} async-done(((bf16[1280,1024]{1,0:T(8,128)(2,1)}), bf16[2560,1024]{1,0:T(8,128)(2,1)}) %all-gather.9.cloned.1.call-update) | async-done | bytes 5242896 | tf_op jit(solution)/shard_map/all_gather | solution.py:22
  87.2 47.4 %all-gather.11.cloned.1.call-done = bf16[3,1024,512]{2,1,0:T(8,128)(2,1)} async-done(((bf16[3,64,512]{2,1,0:T(8,128)(2,1)}), bf16[3,1024,512]{2,1,0:T(8,128)(2,1)}) %all-gather.11.cloned.1.call-update) | async-done | bytes 3145744 | tf_op jit(solution)/shard_map/all_gather | solution.py:31
  134.6 11.3 convolution_bitcast_fusion
  153.2 9.3 fusion.60
  168.4 7.4 squeeze.7
  175.8 7.4 reshape.163
  183.2 6.9 copy.71
  196.0 7.3 squeeze.8
  212.2 16.7 %fusion.13 = (f32[8,8,320]{2,1,0:T(8,128)S(1)}, f32[8,8,320,320]{2,3,1,0:T(8,128)}) fusion(pred[8,320]{1,0:T(8,128)(4,1)S(1)} %iota_compare_fusion, bf16[8,320,8,64]{1,3,2,0:T(8,128)(2,1)S(1)} %copy-done.6, bf16[8,320,8,64]{1,0,3,2:T(8,128)(2,1)} %add_convert_fusion), kind=kOutput, calls=%fused_computation.22 | convolution fusion | flops 858501120 | bytes 31541760 | tf_op jit(solution)/shard_map/bqhe,bkhe->bhqk/dot_general | solution.py:45
  228.9 14.1 fusion
  243.0 16.4 %convert_bitcast_fusion.2 = bf16[8,320,8,64]{1,3,2,0:T(8,128)(2,1)} fusion(f32[8,8,320]{2,1,0:T(8,128)S(1)} %fusion, f32[8,8,320]{2,1,0:T(8,128)S(1)} %get-tuple-element.91, f32[8,8,320,320]{2,3,1,0:T(8,128)} %get-tuple-element.92, pred[8,320]{1,0:T(8,128)(4,1)S(1)} %iota_compare_fusion, bf16[8,320,8,64]{1,0,3,2:T(8,128)(2,1)} %add_convert_fusion.1), kind=kOutput, calls=%fused_computation.69 | convolution fusion | flops 872939520 | bytes 31623680 | tf_op jit(solution)/shard_map/bhqk,bkhe->bqhe/dot_general | solution.py:101
  270.9 8.8 fusion.61
  280.4 120.2 %reduce-scatter.8.cloned.1.call-done = f32[1280,1024]{1,0:T(8,128)} async-done(((f32[2560,1024]{1,0:T(8,128)}), f32[1280,1024]{1,0:T(8,128)}) %reduce-scatter.8.cloned.1.call-update) | async-done | bytes 5242896 | tf_op jit(solution)/shard_map/reduce_scatter | solution.py:26
  409.3 43.9 %all-gather.17.cloned.1.call-done = bf16[1024,2048]{1,0:T(8,128)(2,1)} async-done(((bf16[64,2048]{1,0:T(8,128)(2,1)}), bf16[1024,2048]{1,0:T(8,128)(2,1)}) %all-gather.17.cloned.1.call-update) | async-done | bytes 4194320 | tf_op jit(solution)/shard_map/all_gather | solution.py:38
  453.2 69.1 %all-gather.15.cloned.1.call-done = bf16[2560,1024]{1,0:T(8,128)(2,1)} async-done(((bf16[1280,1024]{1,0:T(8,128)(2,1)}), bf16[2560,1024]{1,0:T(8,128)(2,1)}) %all-gather.15.cloned.1.call-update) | async-done | bytes 5242896 | tf_op jit(solution)/shard_map/all_gather | solution.py:22
  522.3 23.8 %multiply_convert_fusion.1 = (bf16[2560,2048]{1,0:T(8,128)(2,1)}, f32[2560,2048]{1,0:T(8,128)}) fusion(f32[2048]{0:T(1024)S(1)} %copy-done.43, bf16[2560,1024]{1,0:T(8,128)(2,1)} %all-gather.15.cloned.1.call-done, bf16[1024,2048]{1,0:T(8,128)(2,1)} %all-gather.17.cloned.1.call-done), kind=kOutput, calls=%fused_computation.18 | convolution fusion | flops 10789847040 | bytes 40902656 | tf_op jit(solution)/shard_map/dot_general | solution.py:114
  546.1 29.1 %all-gather.19.cloned.1.call-done = bf16[1024,2048]{1,0:T(8,128)(2,1)} async-done(((bf16[64,2048]{1,0:T(8,128)(2,1)}), bf16[1024,2048]{1,0:T(8,128)(2,1)}) %all-gather.19.cloned.1.call-update) | async-done | bytes 4194320 | tf_op jit(solution)/shard_map/all_gather | solution.py:39
  575.2 16.7 %fusion.62 = f32[2560,1024]{1,0:T(8,128)} fusion(bf16[2560,2048]{1,0:T(8,128)(2,1)} %get-tuple-element.93, bf16[1024,2048]{1,0:T(8,128)(2,1)} %all-gather.19.cloned.1.call-done), kind=kOutput, calls=%fused_computation.111 | convolution fusion | flops 10737418240 | bytes 25165824 | tf_op jit(solution)/shard_map/rf,df->rd/dot_general | solution.py:117
  594.0 118.4 %reduce-scatter.10.cloned.1.call-done = f32[1280,1024]{1,0:T(8,128)} async-done(((f32[2560,1024]{1,0:T(8,128)}), f32[1280,1024]{1,0:T(8,128)}) %reduce-scatter.10.cloned.1.call-update) | async-done | bytes 5242896 | tf_op jit(solution)/shard_map/reduce_scatter | solution.py:26
  712.4 6.3 fusion.54
  726.7 68.7 %all-gather.21.cloned.1.call-done = bf16[2560,1024]{1,0:T(8,128)(2,1)} async-done(((bf16[1280,1024]{1,0:T(8,128)(2,1)}), bf16[2560,1024]{1,0:T(8,128)(2,1)}) %all-gather.21.cloned.1.call-update) | async-done | bytes 5242896 | tf_op jit(solution)/shard_map/all_gather | solution.py:22
  795.3 29.0 %convert_reduce_fusion = (f32[2048]{0:T(1024)}, bf16[2560,2048]{1,0:T(8,128)(2,1)S(1)}) fusion(f32[2560,2048]{1,0:T(8,128)} %get-tuple-element.94, f32[2048]{0:T(1024)S(1)} %copy-done.43, bf16[2560,1024]{1,0:T(8,128)(2,1)} %all-gather.21.cloned.1.call-done, bf16[1024,2048]{1,0:T(8,128)(2,1)} %all-gather.19.cloned.1.call-done), kind=kOutput, calls=%fused_computation.17 | convolution fusion | flops 10858002432 | bytes 40910848 | tf_op jit(solution)/shard_map/dot_general | solution.py:126
  828.2 14.5 fusion.63
  842.8 122.0 %reduce-scatter.12.cloned.1.call-done = f32[1280,1024]{1,0:T(8,128)} async-done(((f32[2560,1024]{1,0:T(8,128)}), f32[1280,1024]{1,0:T(8,128)}) %reduce-scatter.12.cloned.1.call-update) | async-done | bytes 5242896 | tf_op jit(solution)/shard_map/reduce_scatter | solution.py:26
  980.0 17.0 %convolution_convert_fusion.1 = bf16[1024,2048]{1,0:T(8,128)(2,1)} fusion(bf16[2560,1024]{1,0:T(8,128)(2,1)} %all-gather.21.cloned.1.call-done, bf16[2560,2048]{1,0:T(8,128)(2,1)} %get-tuple-element.93), kind=kOutput, calls=%fused_computation.63 | convolution fusion | flops 10739515392 | bytes 19922944 | tf_op jit(solution)/shard_map/rd,rf->df/dot_general | solution.py:127
  997.2 16.8 %convolution_convert_fusion.2 = bf16[1024,2048]{1,0:T(8,128)(2,1)} fusion(bf16[2560,1024]{1,0:T(8,128)(2,1)} %all-gather.15.cloned.1.call-done, bf16[2560,2048]{1,0:T(8,128)(2,1)} %copy-done.47), kind=kOutput, calls=%fused_computation.64 | convolution fusion | flops 10739515392 | bytes 19922944 | tf_op jit(solution)/shard_map/rd,rf->df/dot_general | solution.py:130
  1014.3 34.4 %all-gather.23.cloned.1.call-done = bf16[2560,1024]{1,0:T(8,128)(2,1)} async-done(((bf16[1280,1024]{1,0:T(8,128)(2,1)}), bf16[2560,1024]{1,0:T(8,128)(2,1)}) %all-gather.23.cloned.1.call-update) | async-done | bytes 5242896 | tf_op jit(solution)/shard_map/all_gather | solution.py:22
  1058.9 7.2 copy.76
  1066.1 24.7 %multiply_reduce_fusion = (f32[8,8,320]{2,1,0:T(8,128)S(1)}, f32[8,8,320,320]{2,3,1,0:T(8,128)}) fusion(f32[8,8,320]{2,1,0:T(8,128)S(1)} %log_add_fusion, f32[8,8,320,320]{2,3,1,0:T(8,128)} %get-tuple-element.92, pred[8,320]{1,0:T(8,128)(4,1)S(1)} %iota_compare_fusion, bf16[8,320,8,64]{1,3,2,0:T(8,128)(2,1)} %copy.76, bf16[8,320,8,64]{1,0,3,2:T(8,128)(2,1)S(1)} %copy-done.11), kind=kOutput, calls=%fused_computation.1 | convolution fusion | flops 871608320 | bytes 57838080 | tf_op jit(solution)/shard_map/bqhe,bkhe->bhqk/dot_general | solution.py:153
  1090.9 26.7 %multiply_convert_fusion = bf16[8,8,320,320]{2,3,1,0:T(8,128)(2,1)} fusion(f32[8,8,320,320]{2,3,1,0:T(8,128)} %get-tuple-element.96, f32[8,8,320]{2,1,0:T(8,128)S(1)} %get-tuple-element.95, f32[8,8,320]{2,1,0:T(8,128)S(1)} %log_add_fusion, f32[8,8,320,320]{2,3,1,0:T(8,128)} %get-tuple-element.92, pred[8,320]{1,0:T(8,128)(4,1)S(1)} %iota_compare_fusion), kind=kLoop, calls=%fused_computation | loop fusion | flops 39321600 | bytes 65702400 | tf_op jit(solution)/shard_map/convert_element_type | solution.py:159
  1117.6 15.0 convert_reduce_fusion.2
  1132.6 6.9 copy.100
  1139.5 8.2 reshape.161
  1147.7 9.9 fusion.30
  1157.6 6.8 copy.99
  1164.4 8.0 reshape.160
  1172.4 10.3 convert_reduce_fusion.3
  1182.7 6.7 copy.98
  1189.5 8.0 reshape.159
  1203.4 8.8 convert_bitcast_fusion
  1218.2 7.3 convolution_convert_fusion.3
  1225.7 13.0 convolution_bitcast_fusion.1
  1244.4 61.5 %all-reduce.2 = (f32[2,512]{1,0:T(2,128)}, f32[2048]{0:T(1024)}) all-reduce(f32[2,512]{1,0:T(2,128)S(1)} %pad_maximum_fusion, f32[2048]{0:T(1024)S(1)} %copy-done.35), channel_id=1, replica_groups=mesh['dp'=16,'tensor'=2] {'dp'}, use_global_device_ids=true, to_apply=%region_25.26 | all-reduce | flops 3072 | bytes 24576 | tf_op jit(solution)/shard_map/psum | solution.py:213
  1305.9 24.2 %all-reduce.5.cloned.1.call-done = bf16[3,1024,512]{2,0,1:T(4,128)(2,1)} async-done(((bf16[3,1024,512]{2,0,1:T(4,128)(2,1)}), bf16[3,1024,512]{2,0,1:T(4,128)(2,1)}) %all-reduce.5.cloned.1.call-update) | async-done | bytes 3145744
  1332.0 58.4 %reduce-scatter.16.cloned.1.call-done = bf16[64,512]{1,0:T(8,128)(2,1)} async-done(((bf16[1024,512]{1,0:T(8,128)(2,1)}), bf16[64,512]{1,0:T(8,128)(2,1)}) %reduce-scatter.16.cloned.1.call-update) | async-done | bytes 65552 | tf_op jit(solution)/shard_map/reduce_scatter | solution.py:201
  1391.9 121.6 %reduce-scatter.14.cloned.1.call-done = f32[1280,1024]{1,0:T(8,128)} async-done(((f32[2560,1024]{1,0:T(8,128)}), f32[1280,1024]{1,0:T(8,128)}) %reduce-scatter.14.cloned.1.call-update) | async-done | bytes 5242896 | tf_op jit(solution)/shard_map/reduce_scatter | solution.py:26
  1520.6 40.2 %all-reduce.1 = (f32[]{:T(128)}, f32[1024]{0:T(1024)}, f32[1024]{0:T(1024)}, f32[1024]{0:T(1024)}, f32[1024]{0:T(1024)}, /*index=5*/f32[1024]{0:T(1024)}, f32[1024]{0:T(1024)}) all-reduce(f32[]{:T(128)} %get-tuple-element.90, f32[1024]{0:T(1024)S(1)} %get-tuple-element.62, ...), channel_id=1, replica_groups=mesh['dp'=16,'tensor'=2] {'dp','tensor'}, use_global_device_ids=true, to_apply=%region_9.10 | all-reduce | flops 6145 | bytes 49160 | tf_op jit(solution)/shard_map/psum | solution.py:214
  1561.4 6.5 add_add_fusion.2
  (194 shorter events, 125.2 us)
Async XLA Ops:
  7.2 6.2 copy-start.1
  7.2 6.2 copy-start.28
  7.2 6.2 copy-start.36
  7.2 80.0 %all-gather.9.cloned.1.call-start = ((), (), s32[]{:S(2)}) async-start(), calls=%async_computation.7 | async-start | bytes 7864320 | tf_op jit(solution)/shard_map/all_gather | solution.py:22
  9.6 7.7 copy-start.44
  9.6 7.9 copy-start.40
  15.8 118.8 %all-gather.11.cloned.1.call-start = ((), (), s32[]{:S(2)}) async-start(), calls=%async_computation.8 | async-start | bytes 3342336 | tf_op jit(solution)/shard_map/all_gather | solution.py:31
  16.5 254.4 %all-gather.13.cloned.1.call-start = ((), (), s32[]{:S(2)}) async-start(), calls=%async_computation.9 | async-start | bytes 1114112 | tf_op jit(solution)/shard_map/all_gather | solution.py:32
  17.2 383.4 %reduce-scatter.8.cloned.1.call-start = ((), (), s32[]{:S(2)}) async-start(), calls=%async_computation.10 | async-start | bytes 15728640 | tf_op jit(solution)/shard_map/reduce_scatter | solution.py:26
  145.9 5.5 copy-start.13
  203.4 5.8 copy-start.9
  228.9 14.1 copy-start.17
  243.0 16.5 %copy-start.20 = (f32[8,8,320]{2,1,0:T(8,128)}, f32[8,8,320]{2,1,0:T(8,128)S(1)}, u32[]{:S(2)}) copy-start(f32[8,8,320]{2,1,0:T(8,128)S(1)} %fusion) | copy-start | bytes 245764
  279.7 120.9 %copy-start.37 = (f32[1024]{0:T(1024)S(1)}, f32[1024]{0:T(1024)}, u32[]{:S(2)}) copy-start(f32[1024]{0:T(1024)} %param.23) | copy-start | bytes 12292
  279.8 173.5 %all-gather.17.cloned.1.call-start = ((), (), s32[]{:S(2)}) async-start(), calls=%async_computation.12 | async-start | bytes 4456448 | tf_op jit(solution)/shard_map/all_gather | solution.py:38
  280.4 241.9 %all-gather.15.cloned.1.call-start = ((), (), s32[]{:S(2)}) async-start(), calls=%async_computation.11 | async-start | bytes 7864320 | tf_op jit(solution)/shard_map/all_gather | solution.py:22
  406.2 116.1 %copy-start.43 = (f32[2048]{0:T(1024)S(1)}, f32[2048]{0:T(1024)}, u32[]{:S(2)}) copy-start(f32[2048]{0:T(1024)} %param.27) | copy-start | bytes 24580
  408.5 166.7 %all-gather.19.cloned.1.call-start = ((), (), s32[]{:S(2)}) async-start(), calls=%async_computation.13 | async-start | bytes 4456448 | tf_op jit(solution)/shard_map/all_gather | solution.py:39
  409.2 303.2 %reduce-scatter.10.cloned.1.call-start = ((), (), s32[]{:S(2)}) async-start(), calls=%async_computation.14 | async-start | bytes 15728640 | tf_op jit(solution)/shard_map/reduce_scatter | solution.py:26
  591.9 120.6 %copy-start.39 = (f32[1024]{0:T(1024)S(1)}, f32[1024]{0:T(1024)}, u32[]{:S(2)}) copy-start(f32[1024]{0:T(1024)} %param.29) | copy-start | bytes 12292
  591.9 203.4 %all-gather.21.cloned.1.call-start = ((), (), s32[]{:S(2)}) async-start(), calls=%async_computation.15 | async-start | bytes 7864320 | tf_op jit(solution)/shard_map/all_gather | solution.py:22
  594.0 124.8 %copy-start.16 = (bf16[1280,1024]{1,0:T(8,128)(2,1)S(1)}, bf16[1280,1024]{1,0:T(8,128)(2,1)}, u32[]{:S(2)}) copy-start(bf16[1280,1024]{1,0:T(8,128)(2,1)} %param.16) | copy-start | bytes 7864324
  726.6 238.1 %reduce-scatter.12.cloned.1.call-start = ((), (), s32[]{:S(2)}) async-start(), calls=%async_computation.16 | async-start | bytes 15728640 | tf_op jit(solution)/shard_map/reduce_scatter | solution.py:26
  795.3 32.8 %copy-start.41 = (bf16[1024,2048]{1,0:T(8,128)(2,1)S(1)}, bf16[1024,2048]{1,0:T(8,128)(2,1)}, u32[]{:S(2)}) copy-start(bf16[1024,2048]{1,0:T(8,128)(2,1)} %all-gather.17.cloned.1.call-done) | copy-start | bytes 12582916
  842.7 206.0 %all-gather.23.cloned.1.call-start = ((), (), s32[]{:S(2)}) async-start(), calls=%async_computation.17 | async-start | bytes 7864320 | tf_op jit(solution)/shard_map/all_gather | solution.py:22
  964.7 5.8 copy-start.10
  964.7 9.7 slice-start
  980.0 17.2 %copy-start.18 = (f32[8,8,320]{2,1,0:T(8,128)S(1)}, f32[8,8,320]{2,1,0:T(8,128)}, u32[]{:S(2)}) copy-start(f32[8,8,320]{2,1,0:T(8,128)} %copy-done.17) | copy-start | bytes 245764
  980.0 17.2 %copy-start.21 = (f32[8,8,320]{2,1,0:T(8,128)S(1)}, f32[8,8,320]{2,1,0:T(8,128)}, u32[]{:S(2)}) copy-start(f32[8,8,320]{2,1,0:T(8,128)} %copy-done.20) | copy-start | bytes 245764
  980.0 260.6 %reduce-scatter.20.cloned.1.call-start = ((), (), s32[]{:S(2)}) async-start(), calls=%async_computation.21 | async-start | bytes 4456448 | tf_op jit(solution)/shard_map/reduce_scatter | solution.py:209
  997.1 245.3 %reduce-scatter.18.cloned.1.call-start = ((), (), s32[]{:S(2)}) async-start(), calls=%async_computation.20 | async-start | bytes 4456448 | tf_op jit(solution)/shard_map/reduce_scatter | solution.py:206
  1014.1 316.1 %all-reduce.5.cloned.1.call-start = ((), (), s32[]{:S(2)}) async-start(), calls=%async_computation.22 | async-start | bytes 8388608
  1058.9 7.2 copy-start.11
  1090.9 26.7 %copy-start.12 = (bf16[8,320,8,64]{1,3,2,0:T(8,128)(2,1)S(1)}, bf16[8,320,8,64]{1,3,2,0:T(8,128)(2,1)}, u32[]{:S(2)}) copy-start(bf16[8,320,8,64]{1,3,2,0:T(8,128)(2,1)} %copy.76) | copy-start | bytes 7864324
  1139.5 8.2 copy-start.8
  1164.4 8.0 copy-start.7
  1189.5 10.1 copy-start.15
  1197.5 5.9 slice-start.2
  1218.0 7.7 copy-start.42
  1218.0 172.4 %reduce-scatter.16.cloned.1.call-start = ((), (), s32[]{:S(2)}) async-start(), calls=%async_computation.19 | async-start | bytes 1114112 | tf_op jit(solution)/shard_map/reduce_scatter | solution.py:201
  1225.6 287.9 %reduce-scatter.14.cloned.1.call-start = ((), (), s32[]{:S(2)}) async-start(), calls=%async_computation.18 | async-start | bytes 15728640 | tf_op jit(solution)/shard_map/reduce_scatter | solution.py:26
  1238.7 5.7 copy-start.35
  1238.7 274.8 %copy-start.2 = (bf16[1280,1024]{1,0:T(8,128)(2,1)S(1)}, bf16[1280,1024]{1,0:T(8,128)(2,1)}, u32[]{:S(2)}) copy-start(bf16[1280,1024]{1,0:T(8,128)(2,1)} %param.15) | copy-start | bytes 7864324
  1238.7 274.8 %copy-start.23 = (f32[1280]{0:T(1024)S(1)}, f32[1280]{0:T(1024)}, u32[]{:S(2)}) copy-start(f32[1280]{0:T(1024)} %copy-done.22) | copy-start | bytes 15364
  1238.7 274.8 %copy-start.29 = (f32[1024]{0:T(1024)S(1)}, f32[1024]{0:T(1024)}, u32[]{:S(2)}) copy-start(f32[1024]{0:T(1024)} %param.18) | copy-start | bytes 12292
  1242.4 275.0 %copy-start.27 = (f32[1280]{0:T(1024)S(1)}, f32[1280]{0:T(1024)}, u32[]{:S(2)}) copy-start(f32[1280]{0:T(1024)} %copy-done.26) | copy-start | bytes 15364
  1242.4 275.0 %copy-start.25 = (f32[1280]{0:T(1024)S(1)}, f32[1280]{0:T(1024)}, u32[]{:S(2)}) copy-start(f32[1280]{0:T(1024)} %copy-done.24) | copy-start | bytes 15364
  1513.5 4.0 copy-start.4
  (20 other events, 50.7 us)
Sparse Core Ops, SparseCore 0:
  15.9 71.2 all-gather.8
  89.4 45.1 all-gather.10
  136.8 36.7 all-gather.12
  279.9 120.7 reduce-scatter.7
  402.7 50.5 all-gather.16
  455.2 67.0 all-gather.14
  524.5 50.7 all-gather.18
  592.0 120.3 reduce-scatter.9
  726.7 68.5 all-gather.20
  842.8 121.8 reduce-scatter.11
  980.1 68.5 all-gather.22
  1052.4 72.4 reduce-scatter.19
  1129.2 71.3 reduce-scatter.17
  1218.1 111.9 all-reduce.4
  1334.0 56.3 reduce-scatter.15
  1392.5 120.8 reduce-scatter.13
where the time goes:
time: 1590 us; the launch traced here: 1580 us
  waiting for transfers between devices  930 us (58%)
  matrix products  266 us (17%)
  local copies, waits for them, and re-layouts  154 us (10%)
  other arithmetic  105 us (7%)
  blocking collectives  102 us (6%)
  between operations  17.8 us (1%)
    reduce_scatter x4, waiting for transfers between devices, reduce_rows(): return lax.psum_scatter(values, 'tensor', scatter_dimension=0, tiled=True)  482 us
    all_gather x4, waiting for transfers between devices, gather_rows(): return lax.all_gather(values, 'tensor', axis=0, tiled=True)  242 us
    psum x1, blocking collectives, body(): lax.psum((heads_bias_grad, expand_bias_grad), 'dp')  61.5 us
    reduce_scatter x1, waiting for transfers between devices, body(): lax.psum_scatter(merge_grad.astype(jnp.bfloat16), 'dp', scatter_dimension...  58.4 us
    all_gather x1, waiting for transfers between devices, fetch_mixing(): lax.all_gather(query_key_value_weight, 'dp', axis=1, tiled=True)  47.4 us
    another operation x7, local copies, waits for them, and re-layouts, body(): jnp.stack([query_grad.reshape(group_rows, local_width), key_grad.reshape(...  44.8 us
    all_gather x1, waiting for transfers between devices, fetch_feed(): lax.all_gather(expand_weight, 'dp', axis=0, tiled=True)  43.9 us
    psum x1, blocking collectives, body(): lax.psum((first_gain_grad, first_shift_grad, second_gain_grad, second_shi...  40.2 us
  transfers between devices with their start and end apart: 16, of which 13 were waited for; matrix products, arithmetic and copies ran while one was open for 25% of the time, Pallas kernels for 0%

commit v1 on v0

--- a/solution.py
+++ b/solution.py
@@ -11,6 +11,23 @@
 MASKED_SCORE = -1e30
 
 
+def read_halves(message, mesh_ax="dp"):
+    q_n = lax.axis_size(mesh_ax)
+    piece_next = range(q_n)
+    mixed_arr = range(q_n)
+    entries = list(map(lambda ii: (ii, (ii + 1) % q_n), piece_next))
+    r2 = map(lambda ii: (ii, (ii - 1) % q_n), mixed_arr)
+    part_now, b_next = ([message], [message])
+    tray = list(r2)
+    for _ in range(q_n // 2):
+        tmp = lax.ppermute(part_now[-1], mesh_ax, entries)
+        part_now.append(tmp)
+    for _ in range((q_n - 1) // 2):
+        b_next.append(lax.ppermute(b_next[-1], mesh_ax, tray))
+    a_now = jnp.concatenate([*part_now[::-1], *b_next[1:]], 1)
+    return jnp.roll(a_now, (lax.axis_index(mesh_ax) - q_n // 2) * message.shape[1], 1)
+
+
 def layer_norm(rows, gain, shift):
     centre = jnp.mean(rows, axis=-1, keepdims=True)
     centred = rows - centre
@@ -28,7 +45,7 @@
 
 def fetch_mixing(query_key_value_weight, merge_weight):
     return (
-        lax.all_gather(query_key_value_weight, "dp", axis=1, tiled=True),
+        read_halves(query_key_value_weight),
         lax.all_gather(merge_weight, "dp", axis=0, tiled=True),
     )
 

time: 1590 us -> 1540 us (0.969)
  waiting for transfers between devices: 930 us -> 858 us
  starting transfers between devices: 1.04 us -> 41.7 us
  local copies, waits for them, and re-layouts: 154 us -> 132 us
  matrix products: 266 us -> 282 us
    all_gather x4, waiting for transfers between devices: 242 us -> 172 us  [gather_rows(): return lax.all_gather(values, 'tensor', axis=0, tiled=True)]
    all_gather x1 -> x0, waiting for transfers between devices: 47.4 us -> none  [fetch_mixing(): lax.all_gather(query_key_value_weight, 'dp', axis=1, tiled=True)]
    ppermute x0 -> x15, starting transfers between devices: none -> 41.1 us  [the longest x8 26.9 us: read_halves(): tmp = lax.ppermute(part_now[-1], mesh_ax, entries)]
    ppermute x0 -> x15, waiting for transfers between devices: none -> 40.4 us  [the longest x8 40.4 us: read_halves(): tmp = lax.ppermute(part_now[-1], mesh_ax, entries)]
  transfers between devices with their start and end apart: 16 -> 30, of which waited for: 13 -> 19; matrix products, arithmetic and copies ran while one was open for 25% -> 25% of each run, Pallas kernels for 0% -> 0%
where the time goes in v1:
time: 1540 us; the launch traced here: 1530 us
  waiting for transfers between devices  858 us (56%)
  matrix products  282 us (18%)
  local copies, waits for them, and re-layouts  132 us (9%)
  blocking collectives  102 us (7%)
  other arithmetic  99.4 us (6%)
  starting transfers between devices  41.7 us (3%)
  between operations  18 us (1%)
    reduce_scatter x4, waiting for transfers between devices, reduce_rows(): return lax.psum_scatter(values, 'tensor', scatter_dimension=0, tiled=True)  489 us
    all_gather x4, waiting for transfers between devices, gather_rows(): return lax.all_gather(values, 'tensor', axis=0, tiled=True)  172 us
    psum x1, blocking collectives, body(): lax.psum((heads_bias_grad, expand_bias_grad), 'dp')  61.8 us
    reduce_scatter x1, waiting for transfers between devices, body(): lax.psum_scatter(merge_grad.astype(jnp.bfloat16), 'dp', scatter_dimension...  58.4 us
    all_gather x1, waiting for transfers between devices, fetch_feed(): lax.all_gather(expand_weight, 'dp', axis=0, tiled=True)  43.9 us
    another operation x7, local copies, waits for them, and re-layouts, body(): jnp.stack([query_grad.reshape(group_rows, local_width), key_grad.reshape(...  42.8 us
    ppermute x8, waiting for transfers between devices, read_halves(): tmp = lax.ppermute(part_now[-1], mesh_ax, entries)  40.4 us
    psum x1, blocking collectives, body(): lax.psum((first_gain_grad, first_shift_grad, second_gain_grad, second_shi...  40.2 us
  transfers between devices with their start and end apart: 30, of which 19 were waited for; matrix products, arithmetic and copies ran while one was open for 25% of the time, Pallas kernels for 0%

profile of v1, /device:TPU:0, one launch (start us, length us, event | category | flops | bytes accessed | tf_op | source)
XLA Modules:
  0.0 1532.4 jit_solution(8626893869269173160)
XLA Ops:
  76.0 5.9 collective-permute-start.6
  86.2 7.0 collective-permute-start.7
  97.0 8.2 concatenate.7
  105.2 15.5 %convolution_bitcast_fusion = f32[3,2560,512]{1,2,0:T(8,128)} fusion(bf16[2560,1024]{1,0:T(8,128)(2,1)} %all-gather.8.cloned.1.call-done, s32[]{:T(128)S(6)} %select_n.25, bf16[3,1024,512]{1,2,0:T(8,128)(2,1)} %concatenate.7), kind=kOutput, calls=%fused_computation.23 | convolution fusion | flops 8059355136 | bytes 24117252 | tf_op jit(solution)/shard_map/xz,ezi->exi/dot_general | solution.py:103
  124.9 8.8 fusion.65
  133.7 5.9 convert_element_type.127
  139.6 7.3 squeeze.7
  147.0 7.4 squeeze.8
  154.3 16.5 %fusion.13 = (f32[8,8,320]{2,1,0:T(8,128)S(1)}, f32[8,8,320,320]{2,3,1,0:T(8,128)}) fusion(pred[8,320]{1,0:T(8,128)(4,1)S(1)} %iota_compare_fusion, bf16[8,320,8,64]{1,0,3,2:T(8,128)(2,1)} %convert_element_type.127, f32[8,320,8,64]{1,0,3,2:T(8,128)} %squeeze.8, f32[8,64]{1,0:T(8,128)S(1)} %add.165), kind=kOutput, calls=%fused_computation.22 | convolution fusion | flops 861122560 | bytes 34165248 | tf_op jit(solution)/shard_map/bqhe,bkhe->bhqk/dot_general | solution.py:62
  170.8 14.1 fusion
  185.0 17.7 %convert_bitcast_fusion.2 = bf16[8,320,8,64]{1,3,2,0:T(8,128)(2,1)} fusion(f32[8,8,320]{2,1,0:T(8,128)S(1)} %fusion, f32[8,8,320]{2,1,0:T(8,128)S(1)} %get-tuple-element.92, f32[8,8,320,320]{2,3,1,0:T(8,128)} %get-tuple-element.93, pred[8,320]{1,0:T(8,128)(4,1)S(1)} %iota_compare_fusion, f32[8,320,8,64]{1,0,3,2:T(8,128)} %squeeze.7, f32[8,64]{1,0:T(8,128)S(1)} %add.161), kind=kOutput, calls=%fused_computation.74 | convolution fusion | flops 875560960 | bytes 34247168 | tf_op jit(solution)/shard_map/bhqk,bkhe->bqhe/dot_general | solution.py:118
  214.0 8.8 fusion.66
  223.4 127.3 %reduce-scatter.8.cloned.1.call-done = f32[1280,1024]{1,0:T(8,128)} async-done(((f32[2560,1024]{1,0:T(8,128)}), f32[1280,1024]{1,0:T(8,128)}) %reduce-scatter.8.cloned.1.call-update) | async-done | bytes 5242896 | tf_op jit(solution)/shard_map/reduce_scatter | solution.py:43
  359.5 43.9 %all-gather.14.cloned.1.call-done = bf16[1024,2048]{1,0:T(8,128)(2,1)} async-done(((bf16[64,2048]{1,0:T(8,128)(2,1)}), bf16[1024,2048]{1,0:T(8,128)(2,1)}) %all-gather.14.cloned.1.call-update) | async-done | bytes 4194320 | tf_op jit(solution)/shard_map/all_gather | solution.py:55
  403.4 69.1 %all-gather.12.cloned.1.call-done = bf16[2560,1024]{1,0:T(8,128)(2,1)} async-done(((bf16[1280,1024]{1,0:T(8,128)(2,1)}), bf16[2560,1024]{1,0:T(8,128)(2,1)}) %all-gather.12.cloned.1.call-update) | async-done | bytes 5242896 | tf_op jit(solution)/shard_map/all_gather | solution.py:39
  472.5 23.8 %multiply_convert_fusion.1 = (bf16[2560,2048]{1,0:T(8,128)(2,1)}, f32[2560,2048]{1,0:T(8,128)}) fusion(f32[2048]{0:T(1024)S(1)} %copy-done.50, bf16[2560,1024]{1,0:T(8,128)(2,1)} %all-gather.12.cloned.1.call-done, bf16[1024,2048]{1,0:T(8,128)(2,1)} %all-gather.14.cloned.1.call-done), kind=kOutput, calls=%fused_computation.18 | convolution fusion | flops 10789847040 | bytes 40902656 | tf_op jit(solution)/shard_map/dot_general | solution.py:131
  496.3 29.0 %all-gather.16.cloned.1.call-done = bf16[1024,2048]{1,0:T(8,128)(2,1)} async-done(((bf16[64,2048]{1,0:T(8,128)(2,1)}), bf16[1024,2048]{1,0:T(8,128)(2,1)}) %all-gather.16.cloned.1.call-update) | async-done | bytes 4194320 | tf_op jit(solution)/shard_map/all_gather | solution.py:56
  525.2 16.6 %fusion.67 = f32[2560,1024]{1,0:T(8,128)} fusion(bf16[2560,2048]{1,0:T(8,128)(2,1)} %get-tuple-element.94, bf16[1024,2048]{1,0:T(8,128)(2,1)} %all-gather.16.cloned.1.call-done), kind=kOutput, calls=%fused_computation.114 | convolution fusion | flops 10737418240 | bytes 25165824 | tf_op jit(solution)/shard_map/rf,df->rd/dot_general | solution.py:134
  543.9 118.4 %reduce-scatter.10.cloned.1.call-done = f32[1280,1024]{1,0:T(8,128)} async-done(((f32[2560,1024]{1,0:T(8,128)}), f32[1280,1024]{1,0:T(8,128)}) %reduce-scatter.10.cloned.1.call-update) | async-done | bytes 5242896 | tf_op jit(solution)/shard_map/reduce_scatter | solution.py:43
  662.3 6.3 fusion.59
  676.8 68.7 %all-gather.18.cloned.1.call-done = bf16[2560,1024]{1,0:T(8,128)(2,1)} async-done(((bf16[1280,1024]{1,0:T(8,128)(2,1)}), bf16[2560,1024]{1,0:T(8,128)(2,1)}) %all-gather.18.cloned.1.call-update) | async-done | bytes 5242896 | tf_op jit(solution)/shard_map/all_gather | solution.py:39
  745.4 28.8 %convert_reduce_fusion = (f32[2048]{0:T(1024)}, bf16[2560,2048]{1,0:T(8,128)(2,1)S(1)}) fusion(f32[2560,2048]{1,0:T(8,128)} %get-tuple-element.95, f32[2048]{0:T(1024)S(1)} %copy-done.50, bf16[2560,1024]{1,0:T(8,128)(2,1)} %all-gather.18.cloned.1.call-done, bf16[1024,2048]{1,0:T(8,128)(2,1)} %all-gather.16.cloned.1.call-done), kind=kOutput, calls=%fused_computation.17 | convolution fusion | flops 10858002432 | bytes 40910848 | tf_op jit(solution)/shard_map/dot_general | solution.py:143
  778.1 14.3 fusion.68
  792.5 122.0 %reduce-scatter.12.cloned.1.call-done = f32[1280,1024]{1,0:T(8,128)} async-done(((f32[2560,1024]{1,0:T(8,128)}), f32[1280,1024]{1,0:T(8,128)}) %reduce-scatter.12.cloned.1.call-update) | async-done | bytes 5242896 | tf_op jit(solution)/shard_map/reduce_scatter | solution.py:43
  914.5 5.8 multiply_reduce_fusion.1
  929.7 17.0 %convolution_convert_fusion.1 = bf16[1024,2048]{1,0:T(8,128)(2,1)} fusion(bf16[2560,1024]{1,0:T(8,128)(2,1)} %all-gather.18.cloned.1.call-done, bf16[2560,2048]{1,0:T(8,128)(2,1)} %get-tuple-element.94), kind=kOutput, calls=%fused_computation.67 | convolution fusion | flops 10739515392 | bytes 19922944 | tf_op jit(solution)/shard_map/rd,rf->df/dot_general | solution.py:144
  946.9 16.9 %convolution_convert_fusion.2 = bf16[1024,2048]{1,0:T(8,128)(2,1)} fusion(bf16[2560,1024]{1,0:T(8,128)(2,1)} %all-gather.12.cloned.1.call-done, bf16[2560,2048]{1,0:T(8,128)(2,1)} %copy-done.54), kind=kOutput, calls=%fused_computation.68 | convolution fusion | flops 10739515392 | bytes 19922944 | tf_op jit(solution)/shard_map/rd,rf->df/dot_general | solution.py:147
  963.8 34.5 %all-gather.20.cloned.1.call-done = bf16[2560,1024]{1,0:T(8,128)(2,1)} async-done(((bf16[1280,1024]{1,0:T(8,128)(2,1)}), bf16[2560,1024]{1,0:T(8,128)(2,1)}) %all-gather.20.cloned.1.call-update) | async-done | bytes 5242896 | tf_op jit(solution)/shard_map/all_gather | solution.py:39
  1009.0 5.9 copy.79
  1014.9 32.4 %multiply_reduce_fusion = (f32[8,8,320]{2,1,0:T(8,128)S(1)}, f32[8,8,320,320]{2,3,1,0:T(8,128)}) fusion(f32[8,8,320]{2,1,0:T(8,128)S(1)} %log_add_fusion, f32[8,8,320,320]{2,3,1,0:T(8,128)} %get-tuple-element.93, pred[8,320]{1,0:T(8,128)(4,1)S(1)} %iota_compare_fusion, bf16[8,320,8,64]{1,3,2,0:T(8,128)(2,1)S(1)} %copy.79, f32[8,320,8,64]{1,0,3,2:T(8,128)} %squeeze.7, ...), kind=kOutput, calls=%fused_computation.1 | convolution fusion | flops 874229760 | bytes 60461568 | tf_op jit(solution)/shard_map/bqhe,bkhe->bhqk/dot_general | solution.py:170
  1047.3 26.6 %multiply_convert_fusion = bf16[8,8,320,320]{2,3,1,0:T(8,128)(2,1)} fusion(f32[8,8,320,320]{2,3,1,0:T(8,128)} %get-tuple-element.97, f32[8,8,320]{2,1,0:T(8,128)S(1)} %get-tuple-element.96, f32[8,8,320]{2,1,0:T(8,128)S(1)} %log_add_fusion, f32[8,8,320,320]{2,3,1,0:T(8,128)} %get-tuple-element.93, pred[8,320]{1,0:T(8,128)(4,1)S(1)} %iota_compare_fusion), kind=kLoop, calls=%fused_computation | loop fusion | flops 39321600 | bytes 65702400 | tf_op jit(solution)/shard_map/convert_element_type | solution.py:176
  1073.9 15.0 convert_reduce_fusion.2
  1089.0 6.8 copy.103
  1095.8 8.0 reshape.161
  1103.8 10.4 fusion.32
  1119.3 8.0 reshape.160
  1127.3 10.4 convert_reduce_fusion.3
  1137.7 6.7 copy.101
  1144.5 8.0 reshape.159
  1158.3 10.8 convert_bitcast_fusion
  1174.9 7.4 convolution_convert_fusion.3
  1182.4 13.5 convolution_bitcast_fusion.1
  1201.6 61.8 %all-reduce.2 = (f32[2,512]{1,0:T(2,128)}, f32[2048]{0:T(1024)}) all-reduce(f32[2,512]{1,0:T(2,128)S(1)} %pad_maximum_fusion, f32[2048]{0:T(1024)S(1)} %copy-done.43), channel_id=1, replica_groups=mesh['dp'=16,'tensor'=2] {'dp'}, use_global_device_ids=true, to_apply=%region_25.27 | all-reduce | flops 3072 | bytes 24576 | tf_op jit(solution)/shard_map/psum | solution.py:230
  1263.4 23.2 %all-reduce.5.cloned.1.call-done = bf16[3,1024,512]{2,0,1:T(4,128)(2,1)} async-done(((bf16[3,1024,512]{2,0,1:T(4,128)(2,1)}), bf16[3,1024,512]{2,0,1:T(4,128)(2,1)}) %all-reduce.5.cloned.1.call-update) | async-done | bytes 3145744
  1288.5 58.4 %reduce-scatter.16.cloned.1.call-done = bf16[64,512]{1,0:T(8,128)(2,1)} async-done(((bf16[1024,512]{1,0:T(8,128)(2,1)}), bf16[64,512]{1,0:T(8,128)(2,1)}) %reduce-scatter.16.cloned.1.call-update) | async-done | bytes 65552 | tf_op jit(solution)/shard_map/reduce_scatter | solution.py:218
  1348.4 121.6 %reduce-scatter.14.cloned.1.call-done = f32[1280,1024]{1,0:T(8,128)} async-done(((f32[2560,1024]{1,0:T(8,128)}), f32[1280,1024]{1,0:T(8,128)}) %reduce-scatter.14.cloned.1.call-update) | async-done | bytes 5242896 | tf_op jit(solution)/shard_map/reduce_scatter | solution.py:43
  1477.1 40.2 %all-reduce.1 = (f32[]{:T(128)}, f32[1024]{0:T(1024)}, f32[1024]{0:T(1024)}, f32[1024]{0:T(1024)}, f32[1024]{0:T(1024)}, /*index=5*/f32[1024]{0:T(1024)}, f32[1024]{0:T(1024)}) all-reduce(f32[]{:T(128)} %get-tuple-element.91, f32[1024]{0:T(1024)S(1)} %get-tuple-element.63, ...), channel_id=1, replica_groups=mesh['dp'=16,'tensor'=2] {'dp','tensor'}, use_global_device_ids=true, to_apply=%region_9.11 | all-reduce | flops 6145 | bytes 49160 | tf_op jit(solution)/shard_map/psum | solution.py:231
  1517.9 6.5 add_add_fusion.2
  (227 shorter events, 167.1 us)
Async XLA Ops:
  7.2 97.9 %all-gather.8.cloned.1.call-start = ((), (), s32[]{:S(2)}) async-start(), calls=%async_computation.7 | async-start | bytes 7864320 | tf_op jit(solution)/shard_map/all_gather | solution.py:39
  9.6 72.5 %copy-start.48 = (f32[2,512]{1,0:T(2,128)S(1)}, f32[2,512]{1,0:T(2,128)}, u32[]{:S(2)}) copy-start(f32[2,512]{1,0:T(2,128)} %param.23) | copy-start | bytes 12292
  9.6 72.6 %copy-start.51 = (s32[128]{0:T(128)S(1)}, s32[128]{0:T(128)}, u32[]{:S(2)}) copy-start(s32[128]{0:T(128)} %param.19) | copy-start | bytes 1540
  14.7 199.3 %all-gather.10.cloned.1.call-start = ((), (), s32[]{:S(2)}) async-start(), calls=%async_computation.8 | async-start | bytes 1114112 | tf_op jit(solution)/shard_map/all_gather | solution.py:49
  15.0 11.0 collective-permute-start
  15.5 11.5 collective-permute-start.8
  26.0 10.0 collective-permute-start.1
  27.0 11.0 collective-permute-start.9
  36.0 10.0 collective-permute-start.2
  38.0 10.7 collective-permute-start.10
  46.0 10.0 collective-permute-start.3
  48.7 10.7 collective-permute-start.11
  56.0 10.0 collective-permute-start.4
  59.4 11.2 collective-permute-start.12
  66.0 10.0 collective-permute-start.5
  70.6 11.8 collective-permute-start.13
  76.0 10.2 collective-permute-start.6
  82.0 268.8 %reduce-scatter.8.cloned.1.call-start = ((), (), s32[]{:S(2)}) async-start(), calls=%async_computation.9 | async-start | bytes 15728640 | tf_op jit(solution)/shard_map/reduce_scatter | solution.py:43
  82.2 102.8 %copy-start.32 = (f32[8,64]{1,0:T(8,128)}, f32[8,64]{1,0:T(8,128)S(1)}, u32[]{:S(2)}) copy-start(f32[8,64]{1,0:T(8,128)S(1)} %add.161) | copy-start | bytes 6148
  82.3 72.1 %copy-start.27 = (f32[8,64]{1,0:T(8,128)}, f32[8,64]{1,0:T(8,128)S(1)}, u32[]{:S(2)}) copy-start(f32[8,64]{1,0:T(8,128)S(1)} %add.165) | copy-start | bytes 6148
  82.3 11.0 collective-permute-start.14
  86.2 10.7 collective-permute-start.7
  170.8 14.1 copy-start.12
  185.0 17.7 %copy-start.15 = (f32[8,8,320]{2,1,0:T(8,128)}, f32[8,8,320]{2,1,0:T(8,128)S(1)}, u32[]{:S(2)}) copy-start(f32[8,8,320]{2,1,0:T(8,128)S(1)} %fusion) | copy-start | bytes 245764
  222.8 128.0 %copy-start.45 = (f32[1024]{0:T(1024)S(1)}, f32[1024]{0:T(1024)}, u32[]{:S(2)}) copy-start(f32[1024]{0:T(1024)} %param.25) | copy-start | bytes 12292
  222.8 180.6 %all-gather.14.cloned.1.call-start = ((), (), s32[]{:S(2)}) async-start(), calls=%async_computation.11 | async-start | bytes 4456448 | tf_op jit(solution)/shard_map/all_gather | solution.py:55
  223.4 249.1 %all-gather.12.cloned.1.call-start = ((), (), s32[]{:S(2)}) async-start(), calls=%async_computation.10 | async-start | bytes 7864320 | tf_op jit(solution)/shard_map/all_gather | solution.py:39
  356.4 116.1 %copy-start.50 = (f32[2048]{0:T(1024)S(1)}, f32[2048]{0:T(1024)}, u32[]{:S(2)}) copy-start(f32[2048]{0:T(1024)} %param.29) | copy-start | bytes 24580
  358.8 166.4 %all-gather.16.cloned.1.call-start = ((), (), s32[]{:S(2)}) async-start(), calls=%async_computation.12 | async-start | bytes 4456448 | tf_op jit(solution)/shard_map/all_gather | solution.py:56
  359.4 302.9 %reduce-scatter.10.cloned.1.call-start = ((), (), s32[]{:S(2)}) async-start(), calls=%async_computation.13 | async-start | bytes 15728640 | tf_op jit(solution)/shard_map/reduce_scatter | solution.py:43
  541.8 120.5 %copy-start.47 = (f32[1024]{0:T(1024)S(1)}, f32[1024]{0:T(1024)}, u32[]{:S(2)}) copy-start(f32[1024]{0:T(1024)} %param.31) | copy-start | bytes 12292
  541.8 203.6 %all-gather.18.cloned.1.call-start = ((), (), s32[]{:S(2)}) async-start(), calls=%async_computation.14 | async-start | bytes 7864320 | tf_op jit(solution)/shard_map/all_gather | solution.py:39
  543.9 124.7 %copy-start.11 = (bf16[1280,1024]{1,0:T(8,128)(2,1)S(1)}, bf16[1280,1024]{1,0:T(8,128)(2,1)}, u32[]{:S(2)}) copy-start(bf16[1280,1024]{1,0:T(8,128)(2,1)} %param.18) | copy-start | bytes 7864324
  676.7 237.8 %reduce-scatter.12.cloned.1.call-start = ((), (), s32[]{:S(2)}) async-start(), calls=%async_computation.15 | async-start | bytes 15728640 | tf_op jit(solution)/shard_map/reduce_scatter | solution.py:43
  745.4 32.7 %copy-start.49 = (bf16[1024,2048]{1,0:T(8,128)(2,1)S(1)}, bf16[1024,2048]{1,0:T(8,128)(2,1)}, u32[]{:S(2)}) copy-start(bf16[1024,2048]{1,0:T(8,128)(2,1)} %all-gather.14.cloned.1.call-done) | copy-start | bytes 12582916
  792.5 205.9 %all-gather.20.cloned.1.call-start = ((), (), s32[]{:S(2)}) async-start(), calls=%async_computation.16 | async-start | bytes 7864320 | tf_op jit(solution)/shard_map/all_gather | solution.py:39
  929.7 17.2 %copy-start.13 = (f32[8,8,320]{2,1,0:T(8,128)S(1)}, f32[8,8,320]{2,1,0:T(8,128)}, u32[]{:S(2)}) copy-start(f32[8,8,320]{2,1,0:T(8,128)} %copy-done.12) | copy-start | bytes 245764
  929.7 17.2 %copy-start.16 = (f32[8,8,320]{2,1,0:T(8,128)S(1)}, f32[8,8,320]{2,1,0:T(8,128)}, u32[]{:S(2)}) copy-start(f32[8,8,320]{2,1,0:T(8,128)} %copy-done.15) | copy-start | bytes 245764
  929.7 268.1 %reduce-scatter.20.cloned.1.call-start = ((), (), s32[]{:S(2)}) async-start(), calls=%async_computation.20 | async-start | bytes 4456448 | tf_op jit(solution)/shard_map/reduce_scatter | solution.py:226
  946.8 252.8 %reduce-scatter.18.cloned.1.call-start = ((), (), s32[]{:S(2)}) async-start(), calls=%async_computation.19 | async-start | bytes 4456448 | tf_op jit(solution)/shard_map/reduce_scatter | solution.py:223
  963.8 322.8 %all-reduce.5.cloned.1.call-start = ((), (), s32[]{:S(2)}) async-start(), calls=%async_computation.21 | async-start | bytes 8388608
  1174.9 172.0 %reduce-scatter.16.cloned.1.call-start = ((), (), s32[]{:S(2)}) async-start(), calls=%async_computation.18 | async-start | bytes 1114112 | tf_op jit(solution)/shard_map/reduce_scatter | solution.py:218
  1182.3 287.7 %reduce-scatter.14.cloned.1.call-start = ((), (), s32[]{:S(2)}) async-start(), calls=%async_computation.17 | async-start | bytes 15728640 | tf_op jit(solution)/shard_map/reduce_scatter | solution.py:43
  1195.9 274.1 %copy-start.2 = (bf16[1280,1024]{1,0:T(8,128)(2,1)S(1)}, bf16[1280,1024]{1,0:T(8,128)(2,1)}, u32[]{:S(2)}) copy-start(bf16[1280,1024]{1,0:T(8,128)(2,1)} %param.17) | copy-start | bytes 7864324
  1195.9 274.1 %copy-start.26 = (f32[1280]{0:T(1024)S(1)}, f32[1280]{0:T(1024)}, u32[]{:S(2)}) copy-start(f32[1280]{0:T(1024)} %copy-done.25) | copy-start | bytes 15364
  1195.9 274.1 %copy-start.37 = (f32[1024]{0:T(1024)S(1)}, f32[1024]{0:T(1024)}, u32[]{:S(2)}) copy-start(f32[1024]{0:T(1024)} %param.20) | copy-start | bytes 12292
  1199.6 274.2 %copy-start.35 = (f32[1280]{0:T(1024)S(1)}, f32[1280]{0:T(1024)}, u32[]{:S(2)}) copy-start(f32[1280]{0:T(1024)} %copy-done.34) | copy-start | bytes 15364
  1199.6 274.3 %copy-start.31 = (f32[1280]{0:T(1024)S(1)}, f32[1280]{0:T(1024)}, u32[]{:S(2)}) copy-start(f32[1280]{0:T(1024)} %copy-done.30) | copy-start | bytes 15364
  (39 other events, 175.5 us)
Sparse Core Ops, SparseCore 0:
  14.8 71.2 all-gather.7
  88.2 37.9 all-gather.9
  222.9 127.7 reduce-scatter.7
  352.8 50.5 all-gather.13
  405.4 67.0 all-gather.11
  474.5 50.7 all-gather.15
  541.9 120.3 reduce-scatter.9
  676.8 68.5 all-gather.17
  792.6 121.8 reduce-scatter.11
  929.8 68.5 all-gather.19
  1002.2 72.3 reduce-scatter.19
  1078.8 71.7 reduce-scatter.17
  1175.0 111.5 all-reduce.4
  1290.5 56.3 reduce-scatter.15
  1349.1 120.8 reduce-scatter.13
